TPU v7x, 32 devices: a whole 2x2x4 slice. The times are simulated.
32 devices in a mesh: groups: 2 (over y), ctx: 4 (over z), head: 4 (over x, core).
Axes of the slice: x: 2, y: 2, z: 4, core: 2. Of those that a mesh axis runs over, the one named last changes fastest.
Arguments:
- queries: bfloat16 [32768, 2048], P(('groups', 'ctx'), 'head'), parts along dimension 0, may hold values from -6 to 6
- key_vectors: bfloat16 [32768, 2048], P(('groups', 'ctx'), 'head'), parts along dimension 0, may hold values from -0.52734375 to 0.52734375
- value_vectors: bfloat16 [32768, 2048], P(('groups', 'ctx'), 'head'), parts along dimension 0, may hold values from -6 to 6
- token_rows: int32 [32768], P(('groups', 'ctx')), parts along dimension 0, may hold values from 0 to 63
- weight_table: float32 [64, 16, 21], P(None, 'head'), may hold values from 0.1 to 1
Outputs:
- attended: bfloat16 [32768, 2048], P(('groups', 'ctx'), 'head'), parts along dimension 0
There are 2 independent parts, one for each index of `groups`. A program takes and returns all parts, laid end to end along the dimension named above; an argument that names none is the same for every part. Nothing has to cross between parts.
All inputs are finite; a program needn't handle non-finite values.
Results may differ from a plain program's by a relative error of at most 0.004.
Values sent between devices are 32-bit elements; how exact they have to be, the bound alone decides.
A program may use at most 128 MiB of HBM per device.

v0:
```python
import functools

import jax
import jax.numpy as jnp
from jax import lax
from jax.experimental import pallas as pl
from jax.experimental.pallas import tpu as pltpu
from jax.sharding import PartitionSpec as P

BLOCK = 256
HALF = 128
WIDTH = 128
NT = (((1,), (1,)), ((), ()))


def level_constant(level_id):
    return 1.0 if level_id == 0 else 2.0 ** (-(level_id - 1) / 2.0)


def round_up(size, unit):
    return (size + unit - 1) // unit * unit


def node_index(block_count, bit, group):
    start = sum(block_count >> (low + 1) for low in range(bit))
    return start + group


def pair_tile(weight_rows):
    near_row = lax.broadcasted_iota(jnp.int32, (8, HALF), 0)
    near_lane = lax.broadcasted_iota(jnp.int32, (8, HALF), 1)
    near_target = near_lane & 7
    near_xor = near_row ^ near_target
    near = jnp.where(near_xor >= 1, weight_rows[1], weight_rows[0])
    near = jnp.where(near_xor >= 2, weight_rows[2], near)
    near = jnp.where(near_xor >= 4, weight_rows[3], near)
    near = jnp.where(near_row <= near_target, near, 0.0)
    far_row = lax.broadcasted_iota(jnp.int32, (16, HALF), 0)
    far_target = lax.broadcasted_iota(jnp.int32, (16, HALF), 1) >> 3
    far_xor = far_row ^ far_target
    far = jnp.where(far_xor >= 2, weight_rows[5], weight_rows[4])
    far = jnp.where(far_xor >= 4, weight_rows[6], far)
    far = jnp.where(far_xor >= 8, weight_rows[7], far)
    far = jnp.where(far_row <= far_target, far, 0.0)
    lane_group = near_lane >> 3
    return jnp.concatenate(
        [jnp.where(lane_group == row, near, far[row : row + 1]) for row in range(16)], axis=0
    )


def kernel(
    sizes,
    q_hbm,
    k_hbm,
    v_hbm,
    tok_ref,
    tab_ref,
    out_hbm,
    q_v,
    k_v,
    v_v,
    vt_v,
    out_v,
    acc,
    nodes,
    left,
    total,
    lift,
    remote,
    weights,
    table_pad,
    load_sem,
    out_sem,
    send_sem,
    recv_sem,
):
    head_count, block_count, level_count, table_count, shards, device_bits = sizes
    block_bits = BLOCK.bit_length() - 1
    local_bits = block_count.bit_length() - 1
    padded = round_up(level_count, 8)
    me = lax.axis_index("ctx")

    def load(array_id, head_id):
        source = (k_hbm, v_hbm, q_hbm)[array_id]
        target = (k_v, v_v, q_v)[array_id]
        column = pl.multiple_of(head_id * WIDTH, WIDTH)
        return pltpu.make_async_copy(
            source.at[:, pl.ds(column, WIDTH)], target.at[head_id], load_sem.at[array_id, head_id]
        )

    for head_id in range(head_count):
        load(0, head_id).start()
        load(1, head_id).start()
    for head_id in range(head_count):
        load(2, head_id).start()

    if shards > 1:
        barrier = pltpu.get_barrier_semaphore()

        @pl.when(me > 0)
        def _():
            pl.semaphore_signal(
                barrier, inc=1, device_id={"ctx": me - 1}, device_id_type=pl.DeviceIdType.MESH
            )

    level_row = lax.broadcasted_iota(jnp.int32, (padded, WIDTH), 0)
    scale = jnp.zeros((padded, WIDTH), jnp.float32)
    for level_id in range(level_count):
        scale = jnp.where(level_row == level_id, level_constant(level_id), scale)
    table_rows = []
    table_pad[...] = jnp.zeros_like(table_pad)
    for head_id in range(head_count):
        table_pad[0:table_count, 0:level_count] = tab_ref[:, head_id, :]
        table_rows.append(jnp.transpose(table_pad[...])[0:padded] * scale)
    table_all = jnp.concatenate(table_rows, axis=0)
    high = table_all.astype(jnp.bfloat16)
    rest = table_all - high.astype(jnp.float32)
    middle = rest.astype(jnp.bfloat16)
    low = (rest - middle.astype(jnp.float32)).astype(jnp.bfloat16)
    split = jnp.concatenate([high, middle, low], axis=0)
    rows = head_count * padded

    def weigh(block, carry):
        tokens = jnp.concatenate(
            [tok_ref[pl.ds(2 * block, 1), :], tok_ref[pl.ds(2 * block + 1, 1), :]], axis=1
        )
        picks = lax.broadcasted_iota(jnp.int32, (WIDTH, BLOCK), 0) == tokens
        one_hot = jnp.where(picks, 1.0, 0.0).astype(jnp.bfloat16)
        parts = jnp.dot(split, one_hot, preferred_element_type=jnp.float32)
        weights[block] = parts[0:rows] + parts[rows : 2 * rows] + parts[2 * rows :]
        return carry

    lax.fori_loop(0, block_count, weigh, 0)

    def remote_copy(source, bit, head_id):
        return pltpu.make_async_remote_copy(
            src_ref=source,
            dst_ref=remote.at[bit, head_id],
            send_sem=send_sem.at[bit, head_id],
            recv_sem=recv_sem.at[bit, head_id],
            device_id={"ctx": me + 1},
            device_id_type=pl.DeviceIdType.MESH,
        )

    def has_bit(bit):
        return lax.rem(lax.div(me, 2**bit), 2) == 1

    def ends_span(bit):
        return lax.rem(me, 2**bit) == 2**bit - 1

    def is_source(bit):
        return jnp.logical_and(ends_span(bit), jnp.logical_not(has_bit(bit)))

    def is_relay(bit):
        return jnp.logical_and(has_bit(bit), jnp.logical_not(ends_span(bit)))

    if shards > 1:

        @pl.when(me < shards - 1)
        def _():
            pl.semaphore_wait(barrier, 1)

    def states(head_id, carry):
        load(0, head_id).wait()
        load(1, head_id).wait()
        for block in range(block_count):
            span = pl.ds(block * BLOCK, BLOCK)
            value_t = jnp.transpose(v_v[head_id, span, :])
            vt_v[head_id, :, span] = value_t
            state = jnp.dot(value_t, k_v[head_id, span, :], preferred_element_type=jnp.float32)
            bit = 0
            while block >> bit & 1:
                state = left[bit] + state
                bit += 1
            if bit < local_bits:
                left[bit] = state
                nodes[head_id, node_index(block_count, bit, block >> (bit + 1))] = state.astype(
                    jnp.bfloat16
                )
            else:
                total[head_id] = state
        for bit in range(device_bits):

            @pl.when(jnp.logical_not(has_bit(bit)))
            def _(bit=bit):
                remote[bit, head_id] = jnp.zeros((WIDTH, WIDTH), jnp.float32)

        if shards > 1:

            @pl.when(is_source(0))
            def _():
                remote_copy(total.at[head_id], 0, head_id).start()

        return carry

    lax.fori_loop(0, head_count, states, 0)

    def service(bit, head_id):
        @pl.when(has_bit(bit))
        def _():
            remote_copy(total.at[head_id], bit, head_id).wait_recv()

        @pl.when(is_relay(bit))
        def _():
            remote_copy(remote.at[bit, head_id], bit, head_id).start()

        if bit + 1 < device_bits:

            @pl.when(ends_span(bit + 1))
            def _():
                base = total[head_id] if bit == 0 else lift[bit - 1, head_id]
                lift[bit, head_id] = base + remote[bit, head_id]

            @pl.when(is_source(bit + 1))
            def _():
                remote_copy(lift.at[bit, head_id], bit + 1, head_id).start()

    pace = 2 if head_count % 2 == 0 else 1
    steps = head_count // pace

    def weight_row(block, head_id, level_id):
        return weights[block, pl.ds(head_id * padded + level_id, 1), :]

    def inside(head_id, carry):
        load(2, head_id).wait()
        for block in range(block_count):
            if block % (block_count // pace) == 0:
                for bit in range(device_bits):
                    step = head_id - bit

                    @pl.when(jnp.logical_and(step >= 0, step < steps))
                    def _(bit=bit, step=step, block=block):
                        service(bit, step * pace + block // (block_count // pace))

            span = pl.ds(block * BLOCK, BLOCK)
            bits = [bit for bit in range(local_bits) if block >> bit & 1]
            stack = [k_v[head_id, span, :]] + [
                nodes[head_id, node_index(block_count, bit, block >> (bit + 1))] for bit in bits
            ]
            lines = jnp.concatenate(stack, axis=0)
            product = lax.dot_general(
                lines, q_v[head_id, span, :], NT, preferred_element_type=jnp.float32
            )
            level_rows = [
                weight_row(block, head_id, level_id) for level_id in range(block_bits + 1)
            ]
            first = pair_tile([row[:, :HALF] for row in level_rows])
            second = pair_tile([row[:, HALF:] for row in level_rows])
            top = jnp.concatenate(
                [
                    (product[:HALF, :HALF] * first).astype(jnp.bfloat16),
                    (product[:HALF, HALF:] * level_rows[block_bits][:, HALF:]).astype(jnp.bfloat16),
                ],
                axis=1,
            )
            bottom = jnp.concatenate(
                [
                    jnp.zeros((HALF, HALF), jnp.bfloat16),
                    (product[HALF:BLOCK, HALF:] * second).astype(jnp.bfloat16),
                ],
                axis=1,
            )
            weighted = jnp.concatenate([top, bottom], axis=0)
            result = jnp.dot(vt_v[head_id, :, span], weighted, preferred_element_type=jnp.float32)
            for place, bit in enumerate(bits):
                begin = BLOCK + place * WIDTH
                result = result + product[begin : begin + WIDTH] * weight_row(
                    block, head_id, block_bits + 1 + bit
                )
            acc[head_id, block] = result
        return carry

    lax.fori_loop(0, head_count, inside, 0)
    for late in range(head_count, steps + device_bits - 1):
        for bit in range(device_bits):
            step = late - bit
            if 0 <= step < steps:
                for place in range(pace):
                    service(bit, step * pace + place)

    chunk = max(1, block_count // 4)

    def write(head_id, part):
        column = pl.multiple_of(head_id * WIDTH, WIDTH)
        lines = pl.ds(part * chunk * BLOCK, chunk * BLOCK)
        return pltpu.make_async_copy(
            out_v.at[head_id, lines, :],
            out_hbm.at[lines, pl.ds(column, WIDTH)],
            out_sem.at[head_id, part],
        )

    def finish(head_id, carry):
        if device_bits:
            lines = jnp.concatenate(
                [remote[bit, head_id].astype(jnp.bfloat16) for bit in range(device_bits)], axis=0
            )
        for block in range(block_count):
            span = pl.ds(block * BLOCK, BLOCK)
            result = acc[head_id, block]
            if device_bits:
                product = lax.dot_general(
                    lines, q_v[head_id, span, :], NT, preferred_element_type=jnp.float32
                )
            for bit in range(device_bits):
                result = result + product[bit * WIDTH : (bit + 1) * WIDTH] * weight_row(
                    block, head_id, block_bits + local_bits + 1 + bit
                )
            out_v[head_id, span, :] = jnp.transpose(result.astype(jnp.bfloat16))
            if block % chunk == chunk - 1:
                write(head_id, block // chunk).start()
        return carry

    lax.fori_loop(0, head_count, finish, 0)
    for head_id in range(head_count):
        for part in range(block_count // chunk):
            write(head_id, part).wait()
    for bit in range(device_bits):

        @pl.when(jnp.logical_or(is_source(bit), is_relay(bit)))
        def _(bit=bit):
            for head_id in range(head_count):
                remote_copy(total.at[head_id], bit, head_id).wait_send()


def body(queries, key_vectors, value_vectors, token_rows, weight_table):
    table_count, head_count, level_count = weight_table.shape
    token_count = queries.shape[0]
    block_count = token_count // BLOCK
    shards = lax.axis_size("ctx")
    device_bits = shards.bit_length() - 1
    padded = round_up(level_count, 8)
    slots = max(1, device_bits)
    sizes = (head_count, block_count, level_count, table_count, shards, device_bits)
    hbm = pl.BlockSpec(memory_space=pl.ANY)
    vmem = pl.BlockSpec(memory_space=pltpu.VMEM)
    wide = (head_count, token_count, WIDTH)
    state = (WIDTH, WIDTH)
    return pl.pallas_call(
        functools.partial(kernel, sizes),
        out_shape=jax.ShapeDtypeStruct(queries.shape, jnp.bfloat16),
        in_specs=[hbm, hbm, hbm, vmem, vmem],
        out_specs=hbm,
        scratch_shapes=[
            pltpu.VMEM(wide, jnp.bfloat16),
            pltpu.VMEM(wide, jnp.bfloat16),
            pltpu.VMEM(wide, jnp.bfloat16),
            pltpu.VMEM((head_count, WIDTH, token_count), jnp.bfloat16),
            pltpu.VMEM(wide, jnp.bfloat16),
            pltpu.VMEM((head_count, block_count, WIDTH, BLOCK), jnp.float32),
            pltpu.VMEM((head_count, max(1, block_count - 1)) + state, jnp.bfloat16),
            pltpu.VMEM((max(1, block_count.bit_length() - 1),) + state, jnp.float32),
            pltpu.VMEM((head_count,) + state, jnp.float32),
            pltpu.VMEM((slots, head_count) + state, jnp.float32),
            pltpu.VMEM((slots, head_count) + state, jnp.float32),
            pltpu.VMEM((block_count, head_count * padded, BLOCK), jnp.float32),
            pltpu.VMEM((WIDTH, WIDTH), jnp.float32),
            pltpu.SemaphoreType.DMA((3, head_count)),
            pltpu.SemaphoreType.DMA((head_count, 4)),
            pltpu.SemaphoreType.DMA((slots, head_count)),
            pltpu.SemaphoreType.DMA((slots, head_count)),
        ],
        compiler_params=pltpu.CompilerParams(
            collective_id=0, has_side_effects=True, vmem_limit_bytes=48 * 1024 * 1024
        ),
        cost_estimate=pl.CostEstimate(
            flops=10 * token_count * head_count * WIDTH * BLOCK,
            bytes_accessed=8 * token_count * head_count * WIDTH,
            transcendentals=0,
        ),
    )(
        queries,
        key_vectors,
        value_vectors,
        token_rows.reshape(token_count // WIDTH, WIDTH),
        weight_table,
    )


def solution(mesh):
    placed = (
        P(("groups", "ctx"), "head"),
        P(("groups", "ctx"), "head"),
        P(("groups", "ctx"), "head"),
        P(("groups", "ctx")),
        P(None, "head", None),
    )
    return jax.shard_map(
        body, mesh=mesh, in_specs=placed, out_specs=P(("groups", "ctx"), "head"), check_vma=False
    )
```

profile of v0, /device:TPU:28, one launch (start us, length us, event | category | flops | bytes accessed | tf_op | source)
XLA Modules:
  0.0 33.4 jit_solution(14297910558738089064)
XLA Ops:
  0.0 0.9 %copy.6.tab_ref = f32[64,4,21]{2,1,0:T(4,128)S(1)} copy(f32[64,4,21]{0,1,2:T(4,128)} %param.9) | data formatting | bytes 43008 | tf_op args[4]
  0.9 0.0 copy-start
  0.9 0.7 %copy-done = s32[4096]{0:T(1024)S(1)} copy-done((s32[4096]{0:T(1024)S(1)}, s32[4096]{0:T(1024)}, u32[]{:S(2)}) %copy-start) | copy-done | bytes 16408
  1.6 29.8 %shard_map.55 = bf16[4096,512]{1,0:T(8,128)(2,1)S(1)} custom-call(bf16[4096,512]{1,0:T(8,128)(2,1)} %q_hbm.1, bf16[4096,512]{1,0:T(8,128)(2,1)} %k_hbm.1, bf16[4096,512]{1,0:T(8,128)(2,1)} %v_hbm.1, s32[32,128]{1,0:T(8,128)S(1)} %bitcast.1, f32[64,4,21]{2,1,0:T(4,128)S(1)} %copy.6.tab_ref), custom_call_target="tpu_custom_call" | custom-call | flops 5368709120 | bytes 16777216 | tf_op jit(solution)/shard_map/pallas_call | solution.py:338
  31.4 2.0 %copy.8 = bf16[4096,512]{1,0:T(8,128)(2,1)} copy(bf16[4096,512]{1,0:T(8,128)(2,1)S(1)} %shard_map.55) | data formatting | bytes 8388608
Async XLA Ops:
  0.9 0.7 %copy-start = (s32[4096]{0:T(1024)S(1)}, s32[4096]{0:T(1024)}, u32[]{:S(2)}) copy-start(s32[4096]{0:T(1024)} %param.8) | copy-start | bytes 49156
where the time goes:
time: 33.7 us; the launch traced here: 33.4 us
  Pallas kernels  29.8 us (88%)
  local copies, waits for them, and re-layouts  3.63 us (11%)
    pallas_call x1, Pallas kernels, body(): pl.pallas_call(functools.partial(kernel, sizes), out_shape=jax.ShapeDtype...  29.8 us
    unnamed x4, local copies, waits for them, and re-layouts  3.63 us

commit v1 on v0

--- a/solution.py
+++ b/solution.py
@@ -53,23 +53,26 @@
     q_hbm,
     k_hbm,
     v_hbm,
-    tok_ref,
-    tab_ref,
+    tok_hbm,
+    tab_hbm,
     out_hbm,
+    acc,
     q_v,
+    out_v,
+    weights,
     k_v,
     v_v,
     vt_v,
-    out_v,
-    acc,
     nodes,
     left,
     total,
     lift,
-    remote,
-    weights,
+    landed,
+    tok_ref,
+    tab_ref,
     table_pad,
     load_sem,
+    small_sem,
     out_sem,
     send_sem,
     recv_sem,
@@ -88,6 +91,10 @@
             source.at[:, pl.ds(column, WIDTH)], target.at[head_id], load_sem.at[array_id, head_id]
         )
 
+    tokens_in = pltpu.make_async_copy(tok_hbm, tok_ref, small_sem.at[0])
+    table_in = pltpu.make_async_copy(tab_hbm, tab_ref, small_sem.at[1])
+    tokens_in.start()
+    table_in.start()
     for head_id in range(head_count):
         load(0, head_id).start()
         load(1, head_id).start()
@@ -109,9 +116,11 @@
         scale = jnp.where(level_row == level_id, level_constant(level_id), scale)
     table_rows = []
     table_pad[...] = jnp.zeros_like(table_pad)
+    tokens_in.wait()
+    table_in.wait()
     for head_id in range(head_count):
-        table_pad[0:table_count, 0:level_count] = tab_ref[:, head_id, :]
-        table_rows.append(jnp.transpose(table_pad[...])[0:padded] * scale)
+        table_pad[0:level_count, 0:table_count] = tab_ref[:, head_id, :]
+        table_rows.append(table_pad[...] * scale)
     table_all = jnp.concatenate(table_rows, axis=0)
     high = table_all.astype(jnp.bfloat16)
     rest = table_all - high.astype(jnp.float32)
@@ -135,7 +144,7 @@
     def remote_copy(source, bit, head_id):
         return pltpu.make_async_remote_copy(
             src_ref=source,
-            dst_ref=remote.at[bit, head_id],
+            dst_ref=landed.at[bit, head_id],
             send_sem=send_sem.at[bit, head_id],
             recv_sem=recv_sem.at[bit, head_id],
             device_id={"ctx": me + 1},
@@ -163,10 +172,19 @@
     def states(head_id, carry):
         load(0, head_id).wait()
         load(1, head_id).wait()
-        for block in range(block_count):
+
+        def turn(block):
             span = pl.ds(block * BLOCK, BLOCK)
             value_t = jnp.transpose(v_v[head_id, span, :])
             vt_v[head_id, :, span] = value_t
+            return value_t
+
+        value_next = turn(0)
+        for block in range(block_count):
+            span = pl.ds(block * BLOCK, BLOCK)
+            value_t = value_next
+            if block + 1 < block_count:
+                value_next = turn(block + 1)
             state = jnp.dot(value_t, k_v[head_id, span, :], preferred_element_type=jnp.float32)
             bit = 0
             while block >> bit & 1:
@@ -183,7 +201,7 @@
 
             @pl.when(jnp.logical_not(has_bit(bit)))
             def _(bit=bit):
-                remote[bit, head_id] = jnp.zeros((WIDTH, WIDTH), jnp.float32)
+                landed[bit, head_id] = jnp.zeros((WIDTH, WIDTH), jnp.float32)
 
         if shards > 1:
 
@@ -196,51 +214,63 @@
     lax.fori_loop(0, head_count, states, 0)
 
     def service(bit, head_id):
-        @pl.when(has_bit(bit))
+        @pl.when(jnp.logical_and(has_bit(bit), me < shards - 1))
         def _():
             remote_copy(total.at[head_id], bit, head_id).wait_recv()
 
         @pl.when(is_relay(bit))
         def _():
-            remote_copy(remote.at[bit, head_id], bit, head_id).start()
+            remote_copy(landed.at[bit, head_id], bit, head_id).start()
 
         if bit + 1 < device_bits:
 
-            @pl.when(ends_span(bit + 1))
+            @pl.when(jnp.logical_and(ends_span(bit + 1), me < shards - 1))
             def _():
                 base = total[head_id] if bit == 0 else lift[bit - 1, head_id]
-                lift[bit, head_id] = base + remote[bit, head_id]
+                lift[bit, head_id] = base + landed[bit, head_id]
 
             @pl.when(is_source(bit + 1))
             def _():
                 remote_copy(lift.at[bit, head_id], bit + 1, head_id).start()
 
-    pace = 2 if head_count % 2 == 0 else 1
-    steps = head_count // pace
+    segment = block_count // head_count if block_count % head_count == 0 else 0
 
     def weight_row(block, head_id, level_id):
         return weights[block, pl.ds(head_id * padded + level_id, 1), :]
 
     def inside(head_id, carry):
         load(2, head_id).wait()
+
+        def levels_of(block):
+            return [bit for bit in range(local_bits) if block >> bit & 1]
+
+        def multiply(block):
+            span = pl.ds(block * BLOCK, BLOCK)
+            stack = [k_v[head_id, span, :]] + [
+                nodes[head_id, node_index(block_count, bit, block >> (bit + 1))]
+                for bit in levels_of(block)
+            ]
+            return lax.dot_general(
+                jnp.concatenate(stack, axis=0),
+                q_v[head_id, span, :],
+                NT,
+                preferred_element_type=jnp.float32,
+            )
+
+        product_next = multiply(0)
         for block in range(block_count):
-            if block % (block_count // pace) == 0:
-                for bit in range(device_bits):
-                    step = head_id - bit
-
-                    @pl.when(jnp.logical_and(step >= 0, step < steps))
-                    def _(bit=bit, step=step, block=block):
-                        service(bit, step * pace + block // (block_count // pace))
+            if segment and block % segment == 0:
+                for bit in range(min(device_bits, head_count)):
+
+                    @pl.when(head_id == bit)
+                    def _(bit=bit, block=block):
+                        service(bit, block // segment)
 
             span = pl.ds(block * BLOCK, BLOCK)
-            bits = [bit for bit in range(local_bits) if block >> bit & 1]
-            stack = [k_v[head_id, span, :]] + [
-                nodes[head_id, node_index(block_count, bit, block >> (bit + 1))] for bit in bits
-            ]
-            lines = jnp.concatenate(stack, axis=0)
-            product = lax.dot_general(
-                lines, q_v[head_id, span, :], NT, preferred_element_type=jnp.float32
-            )
+            bits = levels_of(block)
+            product = product_next
+            if block + 1 < block_count:
+                product_next = multiply(block + 1)
             level_rows = [
                 weight_row(block, head_id, level_id) for level_id in range(block_bits + 1)
             ]
@@ -271,13 +301,11 @@
         return carry
 
     lax.fori_loop(0, head_count, inside, 0)
-    for late in range(head_count, steps + device_bits - 1):
-        for bit in range(device_bits):
-            step = late - bit
-            if 0 <= step < steps:
-                for place in range(pace):
-                    service(bit, step * pace + place)
-
+    for bit in range(head_count if segment else 0, device_bits):
+        for head_id in range(head_count):
+            service(bit, head_id)
+
+    first_level = BLOCK.bit_length() + block_count.bit_length() - 1
     chunk = max(1, block_count // 4)
 
     def write(head_id, part):
@@ -291,21 +319,38 @@
 
     def finish(head_id, carry):
         if device_bits:
+
+            @pl.when(me == shards - 1)
+            def _():
+                for bit in range(device_bits):
+                    remote_copy(total.at[head_id], bit, head_id).wait_recv()
+
             lines = jnp.concatenate(
-                [remote[bit, head_id].astype(jnp.bfloat16) for bit in range(device_bits)], axis=0
-            )
+                [landed[bit, head_id].astype(jnp.bfloat16) for bit in range(device_bits)], axis=0
+            )
+
+        def multiply(block):
+            if not device_bits:
+                return None
+            return lax.dot_general(
+                lines,
+                q_v[head_id, pl.ds(block * BLOCK, BLOCK), :],
+                NT,
+                preferred_element_type=jnp.float32,
+            )
+
+        product_next = multiply(0)
         for block in range(block_count):
-            span = pl.ds(block * BLOCK, BLOCK)
+            product = product_next
+            if block + 1 < block_count:
+                product_next = multiply(block + 1)
             result = acc[head_id, block]
-            if device_bits:
-                product = lax.dot_general(
-                    lines, q_v[head_id, span, :], NT, preferred_element_type=jnp.float32
-                )
             for bit in range(device_bits):
-                result = result + product[bit * WIDTH : (bit + 1) * WIDTH] * weight_row(
-                    block, head_id, block_bits + local_bits + 1 + bit
-                )
-            out_v[head_id, span, :] = jnp.transpose(result.astype(jnp.bfloat16))
+                row = weights[block, pl.ds(head_id * padded + first_level + bit, 1), :]
+                result = result + product[bit * WIDTH : (bit + 1) * WIDTH] * row
+            out_v[head_id, pl.ds(block * BLOCK, BLOCK), :] = jnp.transpose(
+                result.astype(jnp.bfloat16)
+            )
             if block % chunk == chunk - 1:
                 write(head_id, block // chunk).start()
         return carry
@@ -332,47 +377,54 @@
     slots = max(1, device_bits)
     sizes = (head_count, block_count, level_count, table_count, shards, device_bits)
     hbm = pl.BlockSpec(memory_space=pl.ANY)
-    vmem = pl.BlockSpec(memory_space=pltpu.VMEM)
     wide = (head_count, token_count, WIDTH)
     state = (WIDTH, WIDTH)
     return pl.pallas_call(
         functools.partial(kernel, sizes),
         out_shape=jax.ShapeDtypeStruct(queries.shape, jnp.bfloat16),
-        in_specs=[hbm, hbm, hbm, vmem, vmem],
+        in_specs=[hbm] * 5,
         out_specs=hbm,
         scratch_shapes=[
+            pltpu.VMEM((head_count, block_count, WIDTH, BLOCK), jnp.float32),
             pltpu.VMEM(wide, jnp.bfloat16),
+            pltpu.VMEM(wide, jnp.bfloat16),
+            pltpu.VMEM((block_count, head_count * padded, BLOCK), jnp.float32),
             pltpu.VMEM(wide, jnp.bfloat16),
             pltpu.VMEM(wide, jnp.bfloat16),
             pltpu.VMEM((head_count, WIDTH, token_count), jnp.bfloat16),
-            pltpu.VMEM(wide, jnp.bfloat16),
-            pltpu.VMEM((head_count, block_count, WIDTH, BLOCK), jnp.float32),
             pltpu.VMEM((head_count, max(1, block_count - 1)) + state, jnp.bfloat16),
             pltpu.VMEM((max(1, block_count.bit_length() - 1),) + state, jnp.float32),
             pltpu.VMEM((head_count,) + state, jnp.float32),
             pltpu.VMEM((slots, head_count) + state, jnp.float32),
             pltpu.VMEM((slots, head_count) + state, jnp.float32),
-            pltpu.VMEM((block_count, head_count * padded, BLOCK), jnp.float32),
-            pltpu.VMEM((WIDTH, WIDTH), jnp.float32),
+            pltpu.VMEM((token_count // WIDTH, WIDTH), jnp.int32),
+            pltpu.VMEM((level_count, head_count, table_count), jnp.float32),
+            pltpu.VMEM((padded, WIDTH), jnp.float32),
             pltpu.SemaphoreType.DMA((3, head_count)),
+            pltpu.SemaphoreType.DMA((2,)),
             pltpu.SemaphoreType.DMA((head_count, 4)),
             pltpu.SemaphoreType.DMA((slots, head_count)),
             pltpu.SemaphoreType.DMA((slots, head_count)),
         ],
         compiler_params=pltpu.CompilerParams(
-            collective_id=0, has_side_effects=True, vmem_limit_bytes=48 * 1024 * 1024
+            collective_id=0, has_side_effects=True, vmem_limit_bytes=46 * 1024 * 1024
         ),
         cost_estimate=pl.CostEstimate(
             flops=10 * token_count * head_count * WIDTH * BLOCK,
-            bytes_accessed=8 * token_count * head_count * WIDTH,
+            bytes_accessed=6 * token_count * head_count * WIDTH,
             transcendentals=0,
         ),
     )(
-        queries,
-        key_vectors,
-        value_vectors,
-        token_rows.reshape(token_count // WIDTH, WIDTH),
-        weight_table,
+        *[
+            pltpu.with_memory_space_constraint(operand, pltpu.HBM)
+            for operand in (
+                queries,
+                key_vectors,
+                value_vectors,
+                token_rows.reshape(token_count // WIDTH, WIDTH),
+                weight_table.transpose(2, 1, 0),
+            )
+        ]
     )
 
 

time: 33.7 us -> 32.3 us (0.958)
  the two profiles are of different devices: /device:TPU:28 before, /device:TPU:20 now
where the time goes in v1:
time: 32.3 us; the launch traced here: 32.1 us
  Pallas kernels  30.1 us (93%)
  local copies, waits for them, and re-layouts  2.02 us (6%)
    pallas_call x1, Pallas kernels, body(): pl.pallas_call(functools.partial(kernel, sizes), out_shape=jax.ShapeDtype...  30.1 us
    unnamed x1, local copies, waits for them, and re-layouts  2.02 us

profile of v1, /device:TPU:20, one launch (start us, length us, event | category | flops | bytes accessed | tf_op | source)
XLA Modules:
  0.0 32.1 jit_solution(15333612042228820151)
XLA Ops:
  0.0 30.1 %shard_map.55 = bf16[4096,512]{1,0:T(8,128)(2,1)S(1)} custom-call(bf16[4096,512]{1,0:T(8,128)(2,1)} %q_hbm.1, bf16[4096,512]{1,0:T(8,128)(2,1)} %k_hbm.1, bf16[4096,512]{1,0:T(8,128)(2,1)} %v_hbm.1, s32[32,128]{1,0:T(8,128)} %bitcast.3, f32[21,4,64]{2,1,0:T(4,128)} %bitcast.2), custom_call_target="tpu_custom_call" | custom-call | flops 5368709120 | bytes 12582912 | tf_op jit(solution)/shard_map/pallas_call | solution.py:382
  30.1 2.0 %copy.7 = bf16[4096,512]{1,0:T(8,128)(2,1)} copy(bf16[4096,512]{1,0:T(8,128)(2,1)S(1)} %shard_map.55) | data formatting | bytes 8388608

commit v2 on v1

--- a/solution.py
+++ b/solution.py
@@ -55,10 +55,9 @@
     v_hbm,
     tok_hbm,
     tab_hbm,
-    out_hbm,
     acc,
     q_v,
-    out_v,
+    remote,
     weights,
     k_v,
     v_v,
@@ -73,7 +72,6 @@
     table_pad,
     load_sem,
     small_sem,
-    out_sem,
     send_sem,
     recv_sem,
 ):
@@ -260,9 +258,9 @@
         product_next = multiply(0)
         for block in range(block_count):
             if segment and block % segment == 0:
-                for bit in range(min(device_bits, head_count)):
-
-                    @pl.when(head_id == bit)
+                for bit in range(min(device_bits, head_count - 1)):
+
+                    @pl.when(head_id == bit + 1)
                     def _(bit=bit, block=block):
                         service(bit, block // segment)
 
@@ -301,11 +299,35 @@
         return carry
 
     lax.fori_loop(0, head_count, inside, 0)
-    for bit in range(head_count if segment else 0, device_bits):
+    for bit in range(min(device_bits, head_count - 1) if segment else 0, device_bits):
         for head_id in range(head_count):
             service(bit, head_id)
 
+    if shards > 1:
+
+        @pl.when(me == shards - 1)
+        def _():
+            for bit in range(device_bits):
+                for head_id in range(head_count):
+                    remote_copy(total.at[head_id], bit, head_id).wait_recv()
+
+    for bit in range(device_bits):
+        for head_id in range(head_count):
+            remote[head_id, bit * WIDTH : (bit + 1) * WIDTH, :] = landed[bit, head_id].astype(
+                jnp.bfloat16
+            )
+    for bit in range(device_bits):
+
+        @pl.when(jnp.logical_or(is_source(bit), is_relay(bit)))
+        def _(bit=bit):
+            for head_id in range(head_count):
+                remote_copy(total.at[head_id], bit, head_id).wait_send()
+
+
+def finish_kernel(sizes, acc, q_v, remote, weights, out_hbm, out_v, out_sem):
+    head_count, block_count, level_count, table_count, shards, device_bits = sizes
     first_level = BLOCK.bit_length() + block_count.bit_length() - 1
+    padded = round_up(level_count, 8)
     chunk = max(1, block_count // 4)
 
     def write(head_id, part):
@@ -318,22 +340,11 @@
         )
 
     def finish(head_id, carry):
-        if device_bits:
-
-            @pl.when(me == shards - 1)
-            def _():
-                for bit in range(device_bits):
-                    remote_copy(total.at[head_id], bit, head_id).wait_recv()
-
-            lines = jnp.concatenate(
-                [landed[bit, head_id].astype(jnp.bfloat16) for bit in range(device_bits)], axis=0
-            )
-
         def multiply(block):
             if not device_bits:
                 return None
             return lax.dot_general(
-                lines,
+                remote[head_id],
                 q_v[head_id, pl.ds(block * BLOCK, BLOCK), :],
                 NT,
                 preferred_element_type=jnp.float32,
@@ -359,12 +370,6 @@
     for head_id in range(head_count):
         for part in range(block_count // chunk):
             write(head_id, part).wait()
-    for bit in range(device_bits):
-
-        @pl.when(jnp.logical_or(is_source(bit), is_relay(bit)))
-        def _(bit=bit):
-            for head_id in range(head_count):
-                remote_copy(total.at[head_id], bit, head_id).wait_send()
 
 
 def body(queries, key_vectors, value_vectors, token_rows, weight_table):
@@ -376,19 +381,21 @@
     padded = round_up(level_count, 8)
     slots = max(1, device_bits)
     sizes = (head_count, block_count, level_count, table_count, shards, device_bits)
-    hbm = pl.BlockSpec(memory_space=pl.ANY)
+    hbm = pl.BlockSpec(memory_space=pltpu.HBM)
+    vmem = pl.BlockSpec(memory_space=pltpu.VMEM)
     wide = (head_count, token_count, WIDTH)
     state = (WIDTH, WIDTH)
-    return pl.pallas_call(
+    acc, q_v, remote, weights = pl.pallas_call(
         functools.partial(kernel, sizes),
-        out_shape=jax.ShapeDtypeStruct(queries.shape, jnp.bfloat16),
+        out_shape=[
+            jax.ShapeDtypeStruct((head_count, block_count, WIDTH, BLOCK), jnp.float32),
+            jax.ShapeDtypeStruct(wide, jnp.bfloat16),
+            jax.ShapeDtypeStruct((head_count, slots * WIDTH, WIDTH), jnp.bfloat16),
+            jax.ShapeDtypeStruct((block_count, head_count * padded, BLOCK), jnp.float32),
+        ],
         in_specs=[hbm] * 5,
-        out_specs=hbm,
+        out_specs=[vmem] * 4,
         scratch_shapes=[
-            pltpu.VMEM((head_count, block_count, WIDTH, BLOCK), jnp.float32),
-            pltpu.VMEM(wide, jnp.bfloat16),
-            pltpu.VMEM(wide, jnp.bfloat16),
-            pltpu.VMEM((block_count, head_count * padded, BLOCK), jnp.float32),
             pltpu.VMEM(wide, jnp.bfloat16),
             pltpu.VMEM(wide, jnp.bfloat16),
             pltpu.VMEM((head_count, WIDTH, token_count), jnp.bfloat16),
@@ -402,12 +409,11 @@
             pltpu.VMEM((padded, WIDTH), jnp.float32),
             pltpu.SemaphoreType.DMA((3, head_count)),
             pltpu.SemaphoreType.DMA((2,)),
-            pltpu.SemaphoreType.DMA((head_count, 4)),
             pltpu.SemaphoreType.DMA((slots, head_count)),
             pltpu.SemaphoreType.DMA((slots, head_count)),
         ],
         compiler_params=pltpu.CompilerParams(
-            collective_id=0, has_side_effects=True, vmem_limit_bytes=46 * 1024 * 1024
+            collective_id=0, has_side_effects=True, vmem_limit_bytes=32 * 1024 * 1024
         ),
         cost_estimate=pl.CostEstimate(
             flops=10 * token_count * head_count * WIDTH * BLOCK,
@@ -426,6 +432,22 @@
             )
         ]
     )
+    return pl.pallas_call(
+        functools.partial(finish_kernel, sizes),
+        out_shape=jax.ShapeDtypeStruct(queries.shape, jnp.bfloat16),
+        in_specs=[vmem] * 4,
+        out_specs=hbm,
+        scratch_shapes=[
+            pltpu.VMEM(wide, jnp.bfloat16),
+            pltpu.SemaphoreType.DMA((head_count, 4)),
+        ],
+        compiler_params=pltpu.CompilerParams(vmem_limit_bytes=32 * 1024 * 1024),
+        cost_estimate=pl.CostEstimate(
+            flops=4 * token_count * head_count * WIDTH * WIDTH,
+            bytes_accessed=2 * token_count * head_count * WIDTH,
+            transcendentals=0,
+        ),
+    )(acc, q_v, remote, weights)
 
 
 def solution(mesh):

time: 32.3 us -> 26.7 us (0.83)
  the two profiles are of different devices: /device:TPU:20 before, /device:TPU:22 now
where the time goes in v2:
time: 26.7 us; the launch traced here: 26.6 us
  Pallas kernels  26.6 us (100%)
    pallas_call x1, Pallas kernels, body(): pl.pallas_call(functools.partial(kernel, sizes), out_shape=[jax.ShapeDtyp...  22.5 us
    pallas_call x1, Pallas kernels, body(): pl.pallas_call(functools.partial(finish_kernel, sizes), out_shape=jax.Sha...  4.03 us

profile of v2, /device:TPU:22, one launch (start us, length us, event | category | flops | bytes accessed | tf_op | source)
XLA Modules:
  0.0 26.6 jit_solution(2212716260264794206)
XLA Ops:
  0.0 22.5 %shard_map.55 = (f32[4,16,128,256]{3,2,1,0:T(8,128)S(1)}, bf16[4,4096,128]{2,1,0:T(8,128)(2,1)S(1)}, bf16[4,256,128]{2,1,0:T(8,128)(2,1)S(1)}, f32[16,96,256]{2,1,0:T(8,128)S(1)}) custom-call(bf16[4096,512]{1,0:T(8,128)(2,1)} %q_hbm.1, bf16[4096,512]{1,0:T(8,128)(2,1)} %k_hbm.1, bf16[4096,512]{1,0:T(8,128)(2,1)} %v_hbm.1, s32[32,128]{1,0:T(8,128)} %bitcast.3, ...), custom_call_target="tpu_custom_call" | custom-call | flops 5368709120 | bytes 12582912 | tf_op jit(solution)/shard_map/pallas_call | solution.py:388
  22.5 4.0 %shard_map.56 = bf16[4096,512]{1,0:T(8,128)(2,1)} custom-call(f32[4,16,128,256]{3,2,1,0:T(8,128)S(1)} %get-tuple-element.9.acc, bf16[4,4096,128]{2,1,0:T(8,128)(2,1)S(1)} %get-tuple-element.10.q_v, bf16[4,256,128]{2,1,0:T(8,128)(2,1)S(1)} %get-tuple-element.11.remote, f32[16,96,256]{2,1,0:T(8,128)S(1)} %get-tuple-element.12.weights), custom_call_target="tpu_custom_call" | custom-call | flops 1073741824 | bytes 4194304 | tf_op jit(solution)/shard_map/pallas_call | solution.py:435

commit v3 on v2

--- a/solution.py
+++ b/solution.py
@@ -27,24 +27,23 @@
 
 
 def pair_tile(weight_rows):
-    near_row = lax.broadcasted_iota(jnp.int32, (8, HALF), 0)
-    near_lane = lax.broadcasted_iota(jnp.int32, (8, HALF), 1)
-    near_target = near_lane & 7
-    near_xor = near_row ^ near_target
+    source = lax.broadcasted_iota(jnp.int32, (8, HALF), 0)
+    target = lax.broadcasted_iota(jnp.int32, (8, HALF), 1)
+    near_target = target & 7
+    near_xor = source ^ near_target
     near = jnp.where(near_xor >= 1, weight_rows[1], weight_rows[0])
     near = jnp.where(near_xor >= 2, weight_rows[2], near)
     near = jnp.where(near_xor >= 4, weight_rows[3], near)
-    near = jnp.where(near_row <= near_target, near, 0.0)
-    far_row = lax.broadcasted_iota(jnp.int32, (16, HALF), 0)
-    far_target = lax.broadcasted_iota(jnp.int32, (16, HALF), 1) >> 3
-    far_xor = far_row ^ far_target
-    far = jnp.where(far_xor >= 2, weight_rows[5], weight_rows[4])
-    far = jnp.where(far_xor >= 4, weight_rows[6], far)
-    far = jnp.where(far_xor >= 8, weight_rows[7], far)
-    far = jnp.where(far_row <= far_target, far, 0.0)
-    lane_group = near_lane >> 3
+    near = jnp.where(source <= near_target, near, 0.0)
+    spans = [jnp.zeros((8, HALF), jnp.float32)]
+    for level_id in (7, 6, 5, 4):
+        wider = []
+        for index, span in enumerate(spans):
+            right = target >> (level_id - 1) == 2 * index + 1
+            wider += [jnp.where(right, weight_rows[level_id], span), span]
+        spans = wider
     return jnp.concatenate(
-        [jnp.where(lane_group == row, near, far[row : row + 1]) for row in range(16)], axis=0
+        [jnp.where(target >> 3 == row, near, span) for row, span in enumerate(spans)], axis=0
     )
 
 
@@ -93,11 +92,9 @@
     table_in = pltpu.make_async_copy(tab_hbm, tab_ref, small_sem.at[1])
     tokens_in.start()
     table_in.start()
-    for head_id in range(head_count):
+    for head_id in range(min(2, head_count)):
         load(0, head_id).start()
         load(1, head_id).start()
-    for head_id in range(head_count):
-        load(2, head_id).start()
 
     if shards > 1:
         barrier = pltpu.get_barrier_semaphore()
@@ -127,17 +124,16 @@
     split = jnp.concatenate([high, middle, low], axis=0)
     rows = head_count * padded
 
-    def weigh(block, carry):
+    def weigh(block):
         tokens = jnp.concatenate(
             [tok_ref[pl.ds(2 * block, 1), :], tok_ref[pl.ds(2 * block + 1, 1), :]], axis=1
         )
         picks = lax.broadcasted_iota(jnp.int32, (WIDTH, BLOCK), 0) == tokens
         one_hot = jnp.where(picks, 1.0, 0.0).astype(jnp.bfloat16)
         parts = jnp.dot(split, one_hot, preferred_element_type=jnp.float32)
-        weights[block] = parts[0:rows] + parts[rows : 2 * rows] + parts[2 * rows :]
-        return carry
-
-    lax.fori_loop(0, block_count, weigh, 0)
+        whole = parts[0:rows] + parts[rows : 2 * rows] + parts[2 * rows :]
+        for head_id in range(head_count):
+            weights[block, head_id] = whole[head_id * padded : (head_id + 1) * padded]
 
     def remote_copy(source, bit, head_id):
         return pltpu.make_async_remote_copy(
@@ -171,6 +167,13 @@
         load(0, head_id).wait()
         load(1, head_id).wait()
 
+        @pl.when(head_id + 2 < head_count)
+        def _():
+            load(0, head_id + 2).start()
+            load(1, head_id + 2).start()
+
+        load(2, head_id).start()
+
         def turn(block):
             span = pl.ds(block * BLOCK, BLOCK)
             value_t = jnp.transpose(v_v[head_id, span, :])
@@ -183,6 +186,8 @@
             value_t = value_next
             if block + 1 < block_count:
                 value_next = turn(block + 1)
+            if block % head_count == head_count - 1:
+                weigh(head_id * (block_count // head_count) + block // head_count)
             state = jnp.dot(value_t, k_v[head_id, span, :], preferred_element_type=jnp.float32)
             bit = 0
             while block >> bit & 1:
@@ -231,10 +236,15 @@
             def _():
                 remote_copy(lift.at[bit, head_id], bit + 1, head_id).start()
 
-    segment = block_count // head_count if block_count % head_count == 0 else 0
+    segment = block_count // 4
+    due = sorted(
+        (3 + 5 * bit + 2 * head_id, bit, head_id)
+        for bit in range(device_bits)
+        for head_id in range(head_count)
+    )
 
     def weight_row(block, head_id, level_id):
-        return weights[block, pl.ds(head_id * padded + level_id, 1), :]
+        return weights[block, head_id, level_id : level_id + 1, :]
 
     def inside(head_id, carry):
         load(2, head_id).wait()
@@ -257,12 +267,13 @@
 
         product_next = multiply(0)
         for block in range(block_count):
-            if segment and block % segment == 0:
-                for bit in range(min(device_bits, head_count - 1)):
-
-                    @pl.when(head_id == bit + 1)
-                    def _(bit=bit, block=block):
-                        service(bit, block // segment)
+            if block % segment == 0:
+                for point, bit, which in due:
+                    if point % 4 == block // segment and point < 4 * head_count:
+
+                        @pl.when(head_id == point // 4)
+                        def _(bit=bit, which=which):
+                            service(bit, which)
 
             span = pl.ds(block * BLOCK, BLOCK)
             bits = levels_of(block)
@@ -272,8 +283,8 @@
             level_rows = [
                 weight_row(block, head_id, level_id) for level_id in range(block_bits + 1)
             ]
-            first = pair_tile([row[:, :HALF] for row in level_rows])
-            second = pair_tile([row[:, HALF:] for row in level_rows])
+            first = pair_tile([jnp.broadcast_to(row[:, :HALF], (8, HALF)) for row in level_rows])
+            second = pair_tile([jnp.broadcast_to(row[:, HALF:], (8, HALF)) for row in level_rows])
             top = jnp.concatenate(
                 [
                     (product[:HALF, :HALF] * first).astype(jnp.bfloat16),
@@ -299,8 +310,8 @@
         return carry
 
     lax.fori_loop(0, head_count, inside, 0)
-    for bit in range(min(device_bits, head_count - 1) if segment else 0, device_bits):
-        for head_id in range(head_count):
+    for point, bit, head_id in due:
+        if point >= 4 * head_count:
             service(bit, head_id)
 
     if shards > 1:
@@ -357,7 +368,7 @@
                 product_next = multiply(block + 1)
             result = acc[head_id, block]
             for bit in range(device_bits):
-                row = weights[block, pl.ds(head_id * padded + first_level + bit, 1), :]
+                row = weights[block, head_id, first_level + bit : first_level + bit + 1, :]
                 result = result + product[bit * WIDTH : (bit + 1) * WIDTH] * row
             out_v[head_id, pl.ds(block * BLOCK, BLOCK), :] = jnp.transpose(
                 result.astype(jnp.bfloat16)
@@ -391,7 +402,7 @@
             jax.ShapeDtypeStruct((head_count, block_count, WIDTH, BLOCK), jnp.float32),
             jax.ShapeDtypeStruct(wide, jnp.bfloat16),
             jax.ShapeDtypeStruct((head_count, slots * WIDTH, WIDTH), jnp.bfloat16),
-            jax.ShapeDtypeStruct((block_count, head_count * padded, BLOCK), jnp.float32),
+            jax.ShapeDtypeStruct((block_count, head_count, padded, BLOCK), jnp.float32),
         ],
         in_specs=[hbm] * 5,
         out_specs=[vmem] * 4,

time: 26.7 us -> 22.1 us (0.83)
  the two profiles are of different devices: /device:TPU:22 before, /device:TPU:28 now
where the time goes in v3:
time: 22.1 us; the launch traced here: 22 us
  Pallas kernels  22 us (100%)
    pallas_call x1, Pallas kernels, body(): pl.pallas_call(functools.partial(kernel, sizes), out_shape=[jax.ShapeDtyp...  18 us
    pallas_call x1, Pallas kernels, body(): pl.pallas_call(functools.partial(finish_kernel, sizes), out_shape=jax.Sha...  4.01 us

profile of v3, /device:TPU:28, one launch (start us, length us, event | category | flops | bytes accessed | tf_op | source)
XLA Modules:
  0.0 22.0 jit_solution(6108703808558770303)
XLA Ops:
  0.0 18.0 %shard_map.55 = (f32[4,16,128,256]{3,2,1,0:T(8,128)S(1)}, bf16[4,4096,128]{2,1,0:T(8,128)(2,1)S(1)}, bf16[4,256,128]{2,1,0:T(8,128)(2,1)S(1)}, f32[16,4,24,256]{3,2,1,0:T(8,128)S(1)}) custom-call(bf16[4096,512]{1,0:T(8,128)(2,1)} %q_hbm.1, bf16[4096,512]{1,0:T(8,128)(2,1)} %k_hbm.1, bf16[4096,512]{1,0:T(8,128)(2,1)} %v_hbm.1, s32[32,128]{1,0:T(8,128)} %bitcast.3, ...), custom_call_target="tpu_custom_call" | custom-call | flops 5368709120 | bytes 12582912 | tf_op jit(solution)/shard_map/pallas_call | solution.py:399
  18.0 4.0 %shard_map.56 = bf16[4096,512]{1,0:T(8,128)(2,1)} custom-call(f32[4,16,128,256]{3,2,1,0:T(8,128)S(1)} %get-tuple-element.9.acc, bf16[4,4096,128]{2,1,0:T(8,128)(2,1)S(1)} %get-tuple-element.10.q_v, bf16[4,256,128]{2,1,0:T(8,128)(2,1)S(1)} %get-tuple-element.11.remote, f32[16,4,24,256]{3,2,1,0:T(8,128)S(1)} %get-tuple-element.12.weights), custom_call_target="tpu_custom_call" | custom-call | flops 1073741824 | bytes 4194304 | tf_op jit(solution)/shard_map/pallas_call | solution.py:446

commit v4 on v3

--- a/solution.py
+++ b/solution.py
@@ -238,7 +238,7 @@
 
     segment = block_count // 4
     due = sorted(
-        (3 + 5 * bit + 2 * head_id, bit, head_id)
+        (1 + 5 * bit + 2 * head_id, bit, head_id)
         for bit in range(device_bits)
         for head_id in range(head_count)
     )
@@ -252,34 +252,16 @@
         def levels_of(block):
             return [bit for bit in range(local_bits) if block >> bit & 1]
 
-        def multiply(block):
-            span = pl.ds(block * BLOCK, BLOCK)
-            stack = [k_v[head_id, span, :]] + [
-                nodes[head_id, node_index(block_count, bit, block >> (bit + 1))]
-                for bit in levels_of(block)
-            ]
-            return lax.dot_general(
-                jnp.concatenate(stack, axis=0),
-                q_v[head_id, span, :],
-                NT,
-                preferred_element_type=jnp.float32,
-            )
-
-        product_next = multiply(0)
-        for block in range(block_count):
-            if block % segment == 0:
-                for point, bit, which in due:
-                    if point % 4 == block // segment and point < 4 * head_count:
-
-                        @pl.when(head_id == point // 4)
-                        def _(bit=bit, which=which):
-                            service(bit, which)
-
+        def weigh_pairs(block):
             span = pl.ds(block * BLOCK, BLOCK)
             bits = levels_of(block)
-            product = product_next
-            if block + 1 < block_count:
-                product_next = multiply(block + 1)
+            query = q_v[head_id, span, :]
+            stack = [k_v[head_id, span, :]] + [
+                nodes[head_id, node_index(block_count, bit, block >> (bit + 1))] for bit in bits
+            ]
+            product = lax.dot_general(
+                jnp.concatenate(stack, axis=0), query, NT, preferred_element_type=jnp.float32
+            )
             level_rows = [
                 weight_row(block, head_id, level_id) for level_id in range(block_bits + 1)
             ]
@@ -299,14 +281,34 @@
                 ],
                 axis=1,
             )
-            weighted = jnp.concatenate([top, bottom], axis=0)
-            result = jnp.dot(vt_v[head_id, :, span], weighted, preferred_element_type=jnp.float32)
+            distant = None
             for place, bit in enumerate(bits):
                 begin = BLOCK + place * WIDTH
-                result = result + product[begin : begin + WIDTH] * weight_row(
+                term = product[begin : begin + WIDTH] * weight_row(
                     block, head_id, block_bits + 1 + bit
                 )
-            acc[head_id, block] = result
+                distant = term if distant is None else distant + term
+            return jnp.concatenate([top, bottom], axis=0), distant
+
+        pairs_next = weigh_pairs(0)
+        for block in range(block_count):
+            if block % segment == 0:
+                for point, bit, which in due:
+                    if point % 4 == block // segment and point < 4 * head_count:
+
+                        @pl.when(head_id == point // 4)
+                        def _(bit=bit, which=which):
+                            service(bit, which)
+
+            weighted, distant = pairs_next
+            if block + 1 < block_count:
+                pairs_next = weigh_pairs(block + 1)
+            result = jnp.dot(
+                vt_v[head_id, :, pl.ds(block * BLOCK, BLOCK)],
+                weighted,
+                preferred_element_type=jnp.float32,
+            )
+            acc[head_id, block] = result if distant is None else result + distant
         return carry
 
     lax.fori_loop(0, head_count, inside, 0)
@@ -351,28 +353,26 @@
         )
 
     def finish(head_id, carry):
-        def multiply(block):
-            if not device_bits:
-                return None
-            return lax.dot_general(
-                remote[head_id],
-                q_v[head_id, pl.ds(block * BLOCK, BLOCK), :],
-                NT,
-                preferred_element_type=jnp.float32,
-            )
-
-        product_next = multiply(0)
-        for block in range(block_count):
-            product = product_next
-            if block + 1 < block_count:
-                product_next = multiply(block + 1)
+        def add_up(block):
             result = acc[head_id, block]
+            if device_bits:
+                product = lax.dot_general(
+                    remote[head_id],
+                    q_v[head_id, pl.ds(block * BLOCK, BLOCK), :],
+                    NT,
+                    preferred_element_type=jnp.float32,
+                )
             for bit in range(device_bits):
                 row = weights[block, head_id, first_level + bit : first_level + bit + 1, :]
                 result = result + product[bit * WIDTH : (bit + 1) * WIDTH] * row
-            out_v[head_id, pl.ds(block * BLOCK, BLOCK), :] = jnp.transpose(
-                result.astype(jnp.bfloat16)
-            )
+            return result.astype(jnp.bfloat16)
+
+        result_next = add_up(0)
+        for block in range(block_count):
+            result = result_next
+            if block + 1 < block_count:
+                result_next = add_up(block + 1)
+            out_v[head_id, pl.ds(block * BLOCK, BLOCK), :] = jnp.transpose(result)
             if block % chunk == chunk - 1:
                 write(head_id, block // chunk).start()
         return carry

time: 22.1 us -> 21.6 us (0.977)
  the two profiles are of different devices: /device:TPU:28 before, /device:TPU:0 now
where the time goes in v4:
time: 21.6 us; the launch traced here: 21.5 us
  Pallas kernels  21.5 us (100%)
    pallas_call x1, Pallas kernels, body(): pl.pallas_call(functools.partial(kernel, sizes), out_shape=[jax.ShapeDtyp...  17.5 us
    pallas_call x1, Pallas kernels, body(): pl.pallas_call(functools.partial(finish_kernel, sizes), out_shape=jax.Sha...  4.01 us

profile of v4, /device:TPU:0, one launch (start us, length us, event | category | flops | bytes accessed | tf_op | source)
XLA Modules:
  0.0 21.5 jit_solution(14469932358456438905)
XLA Ops:
  0.0 17.5 %shard_map.55 = (f32[4,16,128,256]{3,2,1,0:T(8,128)S(1)}, bf16[4,4096,128]{2,1,0:T(8,128)(2,1)S(1)}, bf16[4,256,128]{2,1,0:T(8,128)(2,1)S(1)}, f32[16,4,24,256]{3,2,1,0:T(8,128)S(1)}) custom-call(bf16[4096,512]{1,0:T(8,128)(2,1)} %q_hbm.1, bf16[4096,512]{1,0:T(8,128)(2,1)} %k_hbm.1, bf16[4096,512]{1,0:T(8,128)(2,1)} %v_hbm.1, s32[32,128]{1,0:T(8,128)} %bitcast.3, ...), custom_call_target="tpu_custom_call" | custom-call | flops 5368709120 | bytes 12582912 | tf_op jit(solution)/shard_map/pallas_call | solution.py:399
  17.5 4.0 %shard_map.56 = bf16[4096,512]{1,0:T(8,128)(2,1)} custom-call(f32[4,16,128,256]{3,2,1,0:T(8,128)S(1)} %get-tuple-element.9.acc, bf16[4,4096,128]{2,1,0:T(8,128)(2,1)S(1)} %get-tuple-element.10.q_v, bf16[4,256,128]{2,1,0:T(8,128)(2,1)S(1)} %get-tuple-element.11.remote, f32[16,4,24,256]{3,2,1,0:T(8,128)S(1)} %get-tuple-element.12.weights), custom_call_target="tpu_custom_call" | custom-call | flops 1073741824 | bytes 4194304 | tf_op jit(solution)/shard_map/pallas_call | solution.py:446

commit v5 on v4

--- a/solution.py
+++ b/solution.py
@@ -80,12 +80,16 @@
     padded = round_up(level_count, 8)
     me = lax.axis_index("ctx")
 
-    def load(array_id, head_id):
+    half_rows = block_count // 2 * BLOCK
+
+    def load(array_id, head_id, part):
         source = (k_hbm, v_hbm, q_hbm)[array_id]
         target = (k_v, v_v, q_v)[array_id]
         column = pl.multiple_of(head_id * WIDTH, WIDTH)
         return pltpu.make_async_copy(
-            source.at[:, pl.ds(column, WIDTH)], target.at[head_id], load_sem.at[array_id, head_id]
+            source.at[pl.ds(part * half_rows, half_rows), pl.ds(column, WIDTH)],
+            target.at[head_id, pl.ds(part * half_rows, half_rows), :],
+            load_sem.at[array_id, head_id, part],
         )
 
     tokens_in = pltpu.make_async_copy(tok_hbm, tok_ref, small_sem.at[0])
@@ -93,8 +97,9 @@
     tokens_in.start()
     table_in.start()
     for head_id in range(min(2, head_count)):
-        load(0, head_id).start()
-        load(1, head_id).start()
+        for part in range(2):
+            load(1, head_id, part).start()
+            load(0, head_id, part).start()
 
     if shards > 1:
         barrier = pltpu.get_barrier_semaphore()
@@ -157,24 +162,20 @@
     def is_relay(bit):
         return jnp.logical_and(has_bit(bit), jnp.logical_not(ends_span(bit)))
 
-    if shards > 1:
-
-        @pl.when(me < shards - 1)
-        def _():
-            pl.semaphore_wait(barrier, 1)
-
     def states(head_id, carry):
-        load(0, head_id).wait()
-        load(1, head_id).wait()
-
         @pl.when(head_id + 2 < head_count)
         def _():
-            load(0, head_id + 2).start()
-            load(1, head_id + 2).start()
-
-        load(2, head_id).start()
+            for part in range(2):
+                load(1, head_id + 2, part).start()
+                load(0, head_id + 2, part).start()
+
+        for part in range(2):
+            load(2, head_id, part).start()
 
         def turn(block):
+            if block % (block_count // 2) == 0:
+                load(1, head_id, 2 * block // block_count).wait()
+                load(0, head_id, 2 * block // block_count).wait()
             span = pl.ds(block * BLOCK, BLOCK)
             value_t = jnp.transpose(v_v[head_id, span, :])
             vt_v[head_id, :, span] = value_t
@@ -208,6 +209,10 @@
 
         if shards > 1:
 
+            @pl.when(jnp.logical_and(head_id == 0, me < shards - 1))
+            def _():
+                pl.semaphore_wait(barrier, 1)
+
             @pl.when(is_source(0))
             def _():
                 remote_copy(total.at[head_id], 0, head_id).start()
@@ -247,7 +252,8 @@
         return weights[block, head_id, level_id : level_id + 1, :]
 
     def inside(head_id, carry):
-        load(2, head_id).wait()
+        for part in range(2):
+            load(2, head_id, part).wait()
 
         def levels_of(block):
             return [bit for bit in range(local_bits) if block >> bit & 1]
@@ -418,7 +424,7 @@
             pltpu.VMEM((token_count // WIDTH, WIDTH), jnp.int32),
             pltpu.VMEM((level_count, head_count, table_count), jnp.float32),
             pltpu.VMEM((padded, WIDTH), jnp.float32),
-            pltpu.SemaphoreType.DMA((3, head_count)),
+            pltpu.SemaphoreType.DMA((3, head_count, 2)),
             pltpu.SemaphoreType.DMA((2,)),
             pltpu.SemaphoreType.DMA((slots, head_count)),
             pltpu.SemaphoreType.DMA((slots, head_count)),

time: 21.6 us -> 21.2 us (0.981)
  the two profiles are of different devices: /device:TPU:0 before, /device:TPU:28 now
where the time goes in v5:
time: 21.2 us; the launch traced here: 21.1 us
  Pallas kernels  21.1 us (100%)
    pallas_call x1, Pallas kernels, body(): pl.pallas_call(functools.partial(kernel, sizes), out_shape=[jax.ShapeDtyp...  17 us
    pallas_call x1, Pallas kernels, body(): pl.pallas_call(functools.partial(finish_kernel, sizes), out_shape=jax.Sha...  4.02 us

profile of v5, /device:TPU:28, one launch (start us, length us, event | category | flops | bytes accessed | tf_op | source)
XLA Modules:
  0.0 21.1 jit_solution(6143263506681688669)
XLA Ops:
  0.0 17.0 %shard_map.55 = (f32[4,16,128,256]{3,2,1,0:T(8,128)S(1)}, bf16[4,4096,128]{2,1,0:T(8,128)(2,1)S(1)}, bf16[4,256,128]{2,1,0:T(8,128)(2,1)S(1)}, f32[16,4,24,256]{3,2,1,0:T(8,128)S(1)}) custom-call(bf16[4096,512]{1,0:T(8,128)(2,1)} %q_hbm.1, bf16[4096,512]{1,0:T(8,128)(2,1)} %k_hbm.1, bf16[4096,512]{1,0:T(8,128)(2,1)} %v_hbm.1, s32[32,128]{1,0:T(8,128)} %bitcast.3, ...), custom_call_target="tpu_custom_call" | custom-call | flops 5368709120 | bytes 12582912 | tf_op jit(solution)/shard_map/pallas_call | solution.py:405
  17.1 4.0 %shard_map.56 = bf16[4096,512]{1,0:T(8,128)(2,1)} custom-call(f32[4,16,128,256]{3,2,1,0:T(8,128)S(1)} %get-tuple-element.9.acc, bf16[4,4096,128]{2,1,0:T(8,128)(2,1)S(1)} %get-tuple-element.10.q_v, bf16[4,256,128]{2,1,0:T(8,128)(2,1)S(1)} %get-tuple-element.11.remote, f32[16,4,24,256]{3,2,1,0:T(8,128)S(1)} %get-tuple-element.12.weights), custom_call_target="tpu_custom_call" | custom-call | flops 1073741824 | bytes 4194304 | tf_op jit(solution)/shard_map/pallas_call | solution.py:452

commit v6 on v5

--- a/solution.py
+++ b/solution.py
@@ -80,7 +80,7 @@
     padded = round_up(level_count, 8)
     me = lax.axis_index("ctx")
 
-    half_rows = block_count // 2 * BLOCK
+    half_rows = block_count * BLOCK
 
     def load(array_id, head_id, part):
         source = (k_hbm, v_hbm, q_hbm)[array_id]
@@ -97,7 +97,7 @@
     tokens_in.start()
     table_in.start()
     for head_id in range(min(2, head_count)):
-        for part in range(2):
+        for part in range(1):
             load(1, head_id, part).start()
             load(0, head_id, part).start()
 
@@ -165,17 +165,17 @@
     def states(head_id, carry):
         @pl.when(head_id + 2 < head_count)
         def _():
-            for part in range(2):
+            for part in range(1):
                 load(1, head_id + 2, part).start()
                 load(0, head_id + 2, part).start()
 
-        for part in range(2):
+        for part in range(1):
             load(2, head_id, part).start()
 
         def turn(block):
-            if block % (block_count // 2) == 0:
-                load(1, head_id, 2 * block // block_count).wait()
-                load(0, head_id, 2 * block // block_count).wait()
+            if block == 0:
+                load(1, head_id, 0).wait()
+                load(0, head_id, 0).wait()
             span = pl.ds(block * BLOCK, BLOCK)
             value_t = jnp.transpose(v_v[head_id, span, :])
             vt_v[head_id, :, span] = value_t
@@ -241,9 +241,9 @@
             def _():
                 remote_copy(lift.at[bit, head_id], bit + 1, head_id).start()
 
-    segment = block_count // 4
+    segment = block_count // 2
     due = sorted(
-        (1 + 5 * bit + 2 * head_id, bit, head_id)
+        (1 + 2 * bit + head_id, bit, head_id)
         for bit in range(device_bits)
         for head_id in range(head_count)
     )
@@ -252,7 +252,7 @@
         return weights[block, head_id, level_id : level_id + 1, :]
 
     def inside(head_id, carry):
-        for part in range(2):
+        for part in range(1):
             load(2, head_id, part).wait()
 
         def levels_of(block):
@@ -296,16 +296,19 @@
                 distant = term if distant is None else distant + term
             return jnp.concatenate([top, bottom], axis=0), distant
 
+        def pass_on(half):
+            for point, bit, which in due:
+                if point % 2 == half and point < 2 * head_count:
+
+                    @pl.when(head_id == point // 2)
+                    def _(bit=bit, which=which):
+                        service(bit, which)
+
+        pass_on(0)
         pairs_next = weigh_pairs(0)
         for block in range(block_count):
-            if block % segment == 0:
-                for point, bit, which in due:
-                    if point % 4 == block // segment and point < 4 * head_count:
-
-                        @pl.when(head_id == point // 4)
-                        def _(bit=bit, which=which):
-                            service(bit, which)
-
+            if block == segment:
+                pass_on(1)
             weighted, distant = pairs_next
             if block + 1 < block_count:
                 pairs_next = weigh_pairs(block + 1)
@@ -319,7 +322,7 @@
 
     lax.fori_loop(0, head_count, inside, 0)
     for point, bit, head_id in due:
-        if point >= 4 * head_count:
+        if point >= 2 * head_count:
             service(bit, head_id)
 
     if shards > 1:
@@ -424,7 +427,7 @@
             pltpu.VMEM((token_count // WIDTH, WIDTH), jnp.int32),
             pltpu.VMEM((level_count, head_count, table_count), jnp.float32),
             pltpu.VMEM((padded, WIDTH), jnp.float32),
-            pltpu.SemaphoreType.DMA((3, head_count, 2)),
+            pltpu.SemaphoreType.DMA((3, head_count, 1)),
             pltpu.SemaphoreType.DMA((2,)),
             pltpu.SemaphoreType.DMA((slots, head_count)),
             pltpu.SemaphoreType.DMA((slots, head_count)),

time: 21.2 us -> 20.8 us (0.981)
  Pallas kernels: 21.1 us -> 20.6 us
    pallas_call x1, Pallas kernels: 17 us -> 16.6 us  [body(): pl.pallas_call(functools.partial(kernel, sizes), out_shape=[jax.ShapeDtyp...]
where the time goes in v6:
time: 20.8 us; the launch traced here: 20.6 us
  Pallas kernels  20.6 us (99%)
    pallas_call x1, Pallas kernels, body(): pl.pallas_call(functools.partial(kernel, sizes), out_shape=[jax.ShapeDtyp...  16.6 us
    pallas_call x1, Pallas kernels, body(): pl.pallas_call(functools.partial(finish_kernel, sizes), out_shape=jax.Sha...  4.02 us

profile of v6, /device:TPU:28, one launch (start us, length us, event | category | flops | bytes accessed | tf_op | source)
XLA Modules:
  0.0 20.6 jit_solution(15814161172535408681)
XLA Ops:
  0.0 16.6 %shard_map.55 = (f32[4,16,128,256]{3,2,1,0:T(8,128)S(1)}, bf16[4,4096,128]{2,1,0:T(8,128)(2,1)S(1)}, bf16[4,256,128]{2,1,0:T(8,128)(2,1)S(1)}, f32[16,4,24,256]{3,2,1,0:T(8,128)S(1)}) custom-call(bf16[4096,512]{1,0:T(8,128)(2,1)} %q_hbm.1, bf16[4096,512]{1,0:T(8,128)(2,1)} %k_hbm.1, bf16[4096,512]{1,0:T(8,128)(2,1)} %v_hbm.1, s32[32,128]{1,0:T(8,128)} %bitcast.3, ...), custom_call_target="tpu_custom_call" | custom-call | flops 5368709120 | bytes 12582912 | tf_op jit(solution)/shard_map/pallas_call | solution.py:408
  16.6 4.0 %shard_map.56 = bf16[4096,512]{1,0:T(8,128)(2,1)} custom-call(f32[4,16,128,256]{3,2,1,0:T(8,128)S(1)} %get-tuple-element.9.acc, bf16[4,4096,128]{2,1,0:T(8,128)(2,1)S(1)} %get-tuple-element.10.q_v, bf16[4,256,128]{2,1,0:T(8,128)(2,1)S(1)} %get-tuple-element.11.remote, f32[16,4,24,256]{3,2,1,0:T(8,128)S(1)} %get-tuple-element.12.weights), custom_call_target="tpu_custom_call" | custom-call | flops 1073741824 | bytes 4194304 | tf_op jit(solution)/shard_map/pallas_call | solution.py:455

commit v7 on v6

--- a/solution.py
+++ b/solution.py
@@ -243,7 +243,7 @@
 
     segment = block_count // 2
     due = sorted(
-        (1 + 2 * bit + head_id, bit, head_id)
+        (3 * bit + head_id, bit, head_id)
         for bit in range(device_bits)
         for head_id in range(head_count)
     )

time: 20.8 us -> 20.2 us (0.971)
  Pallas kernels: 20.6 us -> 20.1 us
    pallas_call x1, Pallas kernels: 16.6 us -> 16.1 us  [body(): pl.pallas_call(functools.partial(kernel, sizes), out_shape=[jax.ShapeDtyp...]
where the time goes in v7:
time: 20.2 us; the launch traced here: 20.1 us
  Pallas kernels  20.1 us (100%)
    pallas_call x1, Pallas kernels, body(): pl.pallas_call(functools.partial(kernel, sizes), out_shape=[jax.ShapeDtyp...  16.1 us
    pallas_call x1, Pallas kernels, body(): pl.pallas_call(functools.partial(finish_kernel, sizes), out_shape=jax.Sha...  4.02 us

profile of v7, /device:TPU:28, one launch (start us, length us, event | category | flops | bytes accessed | tf_op | source)
XLA Modules:
  0.0 20.1 jit_solution(14364517173961578962)
XLA Ops:
  0.0 16.1 %shard_map.55 = (f32[4,16,128,256]{3,2,1,0:T(8,128)S(1)}, bf16[4,4096,128]{2,1,0:T(8,128)(2,1)S(1)}, bf16[4,256,128]{2,1,0:T(8,128)(2,1)S(1)}, f32[16,4,24,256]{3,2,1,0:T(8,128)S(1)}) custom-call(bf16[4096,512]{1,0:T(8,128)(2,1)} %q_hbm.1, bf16[4096,512]{1,0:T(8,128)(2,1)} %k_hbm.1, bf16[4096,512]{1,0:T(8,128)(2,1)} %v_hbm.1, s32[32,128]{1,0:T(8,128)} %bitcast.3, ...), custom_call_target="tpu_custom_call" | custom-call | flops 5368709120 | bytes 12582912 | tf_op jit(solution)/shard_map/pallas_call | solution.py:408
  16.1 4.0 %shard_map.56 = bf16[4096,512]{1,0:T(8,128)(2,1)} custom-call(f32[4,16,128,256]{3,2,1,0:T(8,128)S(1)} %get-tuple-element.9.acc, bf16[4,4096,128]{2,1,0:T(8,128)(2,1)S(1)} %get-tuple-element.10.q_v, bf16[4,256,128]{2,1,0:T(8,128)(2,1)S(1)} %get-tuple-element.11.remote, f32[16,4,24,256]{3,2,1,0:T(8,128)S(1)} %get-tuple-element.12.weights), custom_call_target="tpu_custom_call" | custom-call | flops 1073741824 | bytes 4194304 | tf_op jit(solution)/shard_map/pallas_call | solution.py:455
